TPU v7x, 32 devices: a whole 2x2x4 slice. The times are simulated.
32 devices in a mesh: row: 4 (over y, x), col: 8 (over z, core).
Axes of the slice: x: 2, y: 2, z: 4, core: 2. Of those that a mesh axis runs over, the one named last changes fastest.
Arguments:
- factor: float32 [4096, 4096], P('row', 'col'), may hold values from -7 to 12
Outputs:
- factor_next: float32 [4096, 4096], P('row', 'col')
All inputs are finite; a program needn't handle non-finite values.
Results may differ from a plain program's by a relative error of at most 0.0078.
Values may be sent and summed in bfloat16 or wider, within the bound.
A program may use at most 64 MiB of HBM per device.

v0:
```python
import functools
import math

import jax
import jax.numpy as jnp
from jax import lax
from jax.experimental import pallas as pl
from jax.experimental.pallas import tpu as pltpu
from jax.sharding import PartitionSpec as P

SWEEPS = 2
STEPS = 2
CHUNKS = 4
MESH = pl.DeviceIdType.MESH


def product(left, right):
    return jnp.dot(left, right, preferred_element_type=jnp.float32)


def product_t(left, right):
    return lax.dot_general(left, right, (((0,), (0,)), ((), ())), preferred_element_type=jnp.float32)


def inner_solve(pair_block):
    size = pair_block.shape[0]
    down = lax.broadcasted_iota(jnp.int32, (size, size), 0)
    across = lax.broadcasted_iota(jnp.int32, (size, size), 1)
    weight_gap = (across - down).astype(jnp.float32) * (0.5 / math.sqrt(size) / size)
    current = pair_block
    rest = None
    for sweep_index in range(SWEEPS):
        trial = current * weight_gap
        trial_low = trial.astype(jnp.bfloat16)
        excess = trial + trial.T + product_t(trial_low, trial_low)
        update = trial - 0.5 * (excess + product(trial_low, excess.astype(jnp.bfloat16)))
        update_low = update.astype(jnp.bfloat16)
        if sweep_index + 1 < SWEEPS:
            half_turned = current + product(current.astype(jnp.bfloat16), update_low)
            current = half_turned + product_t(update_low, half_turned.astype(jnp.bfloat16))
        if rest is None:
            rest = update
        else:
            rest = rest + update + product(rest.astype(jnp.bfloat16), update_low)
    return rest + jnp.where(down == across, 1.0, 0.0)


def kernel(row_count, pair_count, x_ref, o_ref, colr, rowr, gout, gin, hout, hin,
           in_sem, csend, crecv, rsend, rrecv, gsend, grecv, hsend, hrecv):
    width = o_ref.shape[1]
    half = width // 2
    group = o_ref.shape[0] // width
    chunk = width // CHUNKS
    bits = row_count.bit_length() - 1
    row = lax.axis_index("row")
    col = lax.axis_index("col")
    owner_row = col // group
    on_diag = row == owner_row
    slot = col % group
    sibling = col + 1 - 2 * (col % 2)

    load = pltpu.make_async_copy(x_ref, o_ref, in_sem)
    load.start()
    barrier = pltpu.get_barrier_semaphore()
    for offset in range(1, row_count):
        pl.semaphore_signal(barrier, inc=1, device_id={"row": (row + offset) % row_count},
                            device_id_type=MESH)
    for offset in (-2, -1, 1, 2):
        @pl.when((col + offset >= 0) & (col + offset < pair_count))
        def _():
            pl.semaphore_signal(barrier, inc=1, device_id={"col": col + offset}, device_id_type=MESH)
    peers = row_count - 1
    for offset in (-2, -1, 1, 2):
        peers += jnp.where((col + offset >= 0) & (col + offset < pair_count), 1, 0)
    pl.semaphore_wait(barrier, peers)
    load.wait()

    def remote(src, dst, send, recv, where):
        return pltpu.make_async_remote_copy(src_ref=src, dst_ref=dst, send_sem=send, recv_sem=recv,
                                            device_id=where, device_id_type=MESH)

    def act(cond, copy, what):
        @pl.when(cond)
        def _():
            getattr(copy, what)()

    def row_bit(index, bit):
        return (index // (1 << bit)) % 2

    def col_copies(step, q):
        piece = colr.at[step, pl.ds(q * chunk, chunk)]
        order = [(q + i) % bits for i in range(bits)]
        apart = [(row_bit(row, b) + row_bit(owner_row, b)) % 2 for b in order]
        out = []
        for i, b in enumerate(order):
            partner = row + (1 - 2 * row_bit(row, b)) * (1 << b)
            out.append((sum(apart[i:]) == 0,
                        remote(piece, piece, csend.at[step, q, i], crecv.at[step, q], {"row": partner})))
        return out

    def row_copies(step, j, q):
        piece = rowr.at[step, j, pl.ds(q * chunk, chunk)]
        owner = group * row + j
        lane = (col % 2) == (owner % 2)
        recv = rrecv.at[step, j, q]
        return [
            (lane & (col >= owner) & (col + 2 < pair_count),
             remote(piece, piece, rsend.at[step, j, q, 0], recv, {"col": col + 2})),
            (lane & (col <= owner) & (col >= 2),
             remote(piece, piece, rsend.at[step, j, q, 1], recv, {"col": col - 2})),
            (lane, remote(piece, piece, rsend.at[step, j, q, 2], recv, {"col": sibling})),
        ]

    def g_copies(step, j):
        rows = pl.ds(j * width, width)
        return [
            (col + 1 < pair_count,
             remote(gout.at[step, 0, rows], gin.at[step, 0, rows], gsend.at[step, j, 0],
                    grecv.at[step, j, 0], {"col": col + 1})),
            (col > 0,
             remote(gout.at[step, 1, rows], gin.at[step, 1, rows], gsend.at[step, j, 1],
                    grecv.at[step, j, 1], {"col": col - 1})),
        ]

    def h_copies(step):
        return [
            (row + 1 < row_count,
             remote(hout.at[step, 0], hin.at[step, 0], hsend.at[step, 0], hrecv.at[step, 0],
                    {"row": row + 1})),
            (row > 0,
             remote(hout.at[step, 1], hin.at[step, 1], hsend.at[step, 1], hrecv.at[step, 1],
                    {"row": row - 1})),
        ]

    def run(copies, what):
        for cond, copy in copies:
            act(cond, copy, what)

    def relay_col(step, q):
        copies = col_copies(step, q)
        @pl.when(jnp.logical_not(on_diag))
        def _():
            copies[0][1].wait_recv()
            run(copies, "start")

    def relay_row(step, q):
        for j in range(group):
            copies = row_copies(step, j, q)
            @pl.when(col != group * row + j)
            def _():
                copies[2][1].wait_recv()
                run(copies, "start")

    def one_step(step, carry):
        @pl.when(on_diag)
        def _():
            rotation = inner_solve(o_ref[pl.ds(pl.multiple_of(slot * width, width), width), :])
            colr[step] = rotation.astype(jnp.bfloat16)
            for q in range(CHUNKS):
                run(col_copies(step, q), "start")
            rowr[step, slot] = rotation.T.astype(jnp.bfloat16)
            for q in range(CHUNKS):
                for j in range(group):
                    @pl.when(slot == j)
                    def _():
                        run(row_copies(step, j, q), "start")

        for q in range(CHUNKS):
            relay_col(step, q)
            if q + 1 < CHUNKS:
                relay_row(step, q)

        for j in range(group):
            rows = pl.ds(j * width, width)
            right = product(o_ref[rows, :].astype(jnp.bfloat16), colr[step])
            upper = right[:, :half]
            lower = right[:, half:].astype(jnp.bfloat16)
            upper_low = upper.astype(jnp.bfloat16)
            gout[step, 1, rows] = lower

            @pl.when(col == 0)
            def _():
                gout[step, 0, rows] = lower
                gin[step, 0, rows] = upper_low

            @pl.when(col > 0)
            def _():
                gout[step, 0, rows] = upper_low

            @pl.when(col == pair_count - 1)
            def _():
                gin[step, 1, rows] = upper_low

            run(g_copies(step, j), "start")
        relay_row(step, CHUNKS - 1)

        for j in [0, group - 1] + list(range(1, group - 1)):
            rows = pl.ds(j * width, width)
            copies = g_copies(step, j)
            act(col > 0, copies[0][1], "wait_recv")
            act(col + 1 < pair_count, copies[1][1], "wait_recv")
            left = rowr[step, j]
            upper_rows = []
            for side in range(2):
                rotated = product(left, gin[step, side, rows])
                cols = pl.ds(side * half, half)
                upper = rotated[:half]
                lower = rotated[half:]

                def put(index, block):
                    o_ref[pl.ds(index * half, half), cols] = block

                if j == 0:
                    @pl.when(row == 0)
                    def _():
                        put(0, upper)
                        put(2, lower)

                    @pl.when(row > 0)
                    def _():
                        put(2, upper)
                        hout[step, 1, :, cols] = lower.astype(jnp.bfloat16)
                else:
                    put(2 * j - 1, lower)
                    if j < group - 1:
                        put(2 * j + 2, upper)
                    else:
                        @pl.when(row == row_count - 1)
                        def _():
                            put(2 * j + 1, upper)

                        @pl.when(row < row_count - 1)
                        def _():
                            hout[step, 0, :, cols] = upper.astype(jnp.bfloat16)
            if j == 0:
                run(h_copies(step)[1:], "start")
            elif j == group - 1:
                run(h_copies(step)[:1], "start")

        copies = h_copies(step)

        @pl.when(row < row_count - 1)
        def _():
            copies[1][1].wait_recv()
            o_ref[pl.ds((2 * group - 1) * half, half), :] = hin[step, 1].astype(jnp.float32)

        @pl.when(row > 0)
        def _():
            copies[0][1].wait_recv()
            o_ref[pl.ds(0, half), :] = hin[step, 0].astype(jnp.float32)

        for q in range(CHUNKS):
            run(col_copies(step, q), "wait_send")
            for j in range(group):
                run(row_copies(step, j, q), "wait_send")
        for j in range(group):
            run(g_copies(step, j), "wait_send")
        run(copies, "wait_send")
        return carry

    lax.fori_loop(0, STEPS, one_step, 0)


def shards(factor):
    rows, width = factor.shape
    half = width // 2
    group = rows // width
    row_count = lax.axis_size("row")
    pair_count = lax.axis_size("col")
    bits = row_count.bit_length() - 1
    low = jnp.bfloat16
    dma = pltpu.SemaphoreType.DMA
    return pl.pallas_call(
        functools.partial(kernel, row_count, pair_count),
        out_shape=jax.ShapeDtypeStruct(factor.shape, factor.dtype),
        in_specs=[pl.BlockSpec(memory_space=pl.ANY)],
        out_specs=pl.BlockSpec(memory_space=pltpu.VMEM),
        scratch_shapes=[
            pltpu.VMEM((STEPS, width, width), low),
            pltpu.VMEM((STEPS, group, width, width), low),
            pltpu.VMEM((STEPS, 2, rows, half), low),
            pltpu.VMEM((STEPS, 2, rows, half), low),
            pltpu.VMEM((STEPS, 2, half, width), low),
            pltpu.VMEM((STEPS, 2, half, width), low),
            dma,
            dma((STEPS, CHUNKS, bits)),
            dma((STEPS, CHUNKS)),
            dma((STEPS, group, CHUNKS, 3)),
            dma((STEPS, group, CHUNKS)),
            dma((STEPS, group, 2)),
            dma((STEPS, group, 2)),
            dma((STEPS, 2)),
            dma((STEPS, 2)),
        ],
        compiler_params=pltpu.CompilerParams(
            collective_id=0, has_side_effects=True, vmem_limit_bytes=56 * 1024 * 1024
        ),
    )(factor)


def solution(mesh):
    spec = P("row", "col")
    return jax.shard_map(shards, mesh=mesh, in_specs=(spec,), out_specs=spec, check_vma=False)
```

profile of v0, /device:TPU:6, one launch (start us, length us, event | category | flops | bytes accessed | tf_op | source)
XLA Modules:
  0.0 98.4 jit_solution(17530306476891993959)
XLA Ops:
  0.0 95.3 %shard_map.17 = f32[1024,512]{1,0:T(8,128)} custom-call(f32[1024,512]{1,0:T(8,128)} %x_ref.1), custom_call_target="tpu_custom_call" | custom-call | tf_op jit(solution)/shard_map/pallas_call | solution.py:273
  95.3 3.1 %copy.3 = f32[1024,512]{1,0:T(8,128)} copy(f32[1024,512]{1,0:T(8,128)} %shard_map.17) | data formatting | bytes 4194304
where the time goes:
time: 98.5 us; the launch traced here: 98.4 us
  Pallas kernels  95.3 us (97%)
  local copies, waits for them, and re-layouts  3.08 us (3%)
    pallas_call x1, Pallas kernels, shards(): pl.pallas_call(functools.partial(kernel, row_count, pair_count), out_shap...  95.3 us
    unnamed x1, local copies, waits for them, and re-layouts  3.08 us

commit v1 on v0

--- a/solution.py
+++ b/solution.py
@@ -11,6 +11,7 @@
 SWEEPS = 2
 STEPS = 2
 CHUNKS = 4
+PARTS = 1
 MESH = pl.DeviceIdType.MESH
 
 
@@ -46,11 +47,13 @@
 
 
 def kernel(row_count, pair_count, x_ref, o_ref, colr, rowr, gout, gin, hout, hin,
-           in_sem, csend, crecv, rsend, rrecv, gsend, grecv, hsend, hrecv):
+           in_sem, csend, crecv, rsend, rrecv, tsend, trecv, gsend, grecv, hsend, hrecv):
     width = o_ref.shape[1]
     half = width // 2
     group = o_ref.shape[0] // width
     chunk = width // CHUNKS
+    parts = csend.shape[1]
+    part = width // parts
     bits = row_count.bit_length() - 1
     row = lax.axis_index("row")
     col = lax.axis_index("col")
@@ -72,8 +75,6 @@
     peers = row_count - 1
     for offset in (-2, -1, 1, 2):
         peers += jnp.where((col + offset >= 0) & (col + offset < pair_count), 1, 0)
-    pl.semaphore_wait(barrier, peers)
-    load.wait()
 
     def remote(src, dst, send, recv, where):
         return pltpu.make_async_remote_copy(src_ref=src, dst_ref=dst, send_sem=send, recv_sem=recv,
@@ -88,7 +89,7 @@
         return (index // (1 << bit)) % 2
 
     def col_copies(step, q):
-        piece = colr.at[step, pl.ds(q * chunk, chunk)]
+        piece = colr.at[step, pl.ds(q * part, part)]
         order = [(q + i) % bits for i in range(bits)]
         apart = [(row_bit(row, b) + row_bit(owner_row, b)) % 2 for b in order]
         out = []
@@ -98,18 +99,23 @@
                         remote(piece, piece, csend.at[step, q, i], crecv.at[step, q], {"row": partner})))
         return out
 
+    def on_lane(j):
+        return (col % 2) == ((group * row + j) % 2)
+
     def row_copies(step, j, q):
         piece = rowr.at[step, j, pl.ds(q * chunk, chunk)]
         owner = group * row + j
-        lane = (col % 2) == (owner % 2)
         recv = rrecv.at[step, j, q]
         return [
-            (lane & (col >= owner) & (col + 2 < pair_count),
+            (on_lane(j) & (col >= owner) & (col + 2 < pair_count),
              remote(piece, piece, rsend.at[step, j, q, 0], recv, {"col": col + 2})),
-            (lane & (col <= owner) & (col >= 2),
+            (on_lane(j) & (col <= owner) & (col >= 2),
              remote(piece, piece, rsend.at[step, j, q, 1], recv, {"col": col - 2})),
-            (lane, remote(piece, piece, rsend.at[step, j, q, 2], recv, {"col": sibling})),
         ]
+
+    def twin_copy(step, j):
+        piece = rowr.at[step, j]
+        return remote(piece, piece, tsend.at[step, j], trecv.at[step, j], {"col": sibling})
 
     def g_copies(step, j):
         rows = pl.ds(j * width, width)
@@ -136,39 +142,78 @@
         for cond, copy in copies:
             act(cond, copy, what)
 
-    def relay_col(step, q):
-        copies = col_copies(step, q)
-        @pl.when(jnp.logical_not(on_diag))
-        def _():
-            copies[0][1].wait_recv()
-            run(copies, "start")
+    def relay_col(step):
+        for q in range(parts):
+            copies = col_copies(step, q)
+            @pl.when(jnp.logical_not(on_diag) & copies[-1][0])
+            def _():
+                copies[0][1].wait_recv()
+                run(copies, "start")
+
+    def settle_col(step):
+        for q in range(parts):
+            copies = col_copies(step, q)
+            @pl.when(jnp.logical_not(on_diag | copies[-1][0]))
+            def _():
+                copies[0][1].wait_recv()
 
     def relay_row(step, q):
         for j in range(group):
             copies = row_copies(step, j, q)
-            @pl.when(col != group * row + j)
-            def _():
-                copies[2][1].wait_recv()
+            @pl.when(on_lane(j) & (col != group * row + j))
+            def _():
+                copies[0][1].wait_recv()
                 run(copies, "start")
+                if q == CHUNKS - 1:
+                    twin_copy(step, j).start()
+
+    def receive_rows(step):
+        copies = h_copies(step)
+
+        @pl.when(row < row_count - 1)
+        def _():
+            copies[1][1].wait_recv()
+            o_ref[pl.ds((2 * group - 1) * half, half), :] = hin[step, 1].astype(jnp.float32)
+
+        @pl.when(row > 0)
+        def _():
+            copies[0][1].wait_recv()
+            o_ref[pl.ds(0, half), :] = hin[step, 0].astype(jnp.float32)
+
+    def solve(step):
+        rotation = inner_solve(o_ref[pl.ds(pl.multiple_of(slot * width, width), width), :])
+        colr[step] = rotation.astype(jnp.bfloat16)
+        rowr[step, slot] = rotation.T.astype(jnp.bfloat16)
+
+    load.wait()
+
+    @pl.when(on_diag)
+    def _():
+        solve(0)
+
+    pl.semaphore_wait(barrier, peers)
 
     def one_step(step, carry):
         @pl.when(on_diag)
         def _():
-            rotation = inner_solve(o_ref[pl.ds(pl.multiple_of(slot * width, width), width), :])
-            colr[step] = rotation.astype(jnp.bfloat16)
-            for q in range(CHUNKS):
-                run(col_copies(step, q), "start")
-            rowr[step, slot] = rotation.T.astype(jnp.bfloat16)
-            for q in range(CHUNKS):
-                for j in range(group):
-                    @pl.when(slot == j)
-                    def _():
+            for i in range(bits):
+                for q in range(parts):
+                    col_copies(step, q)[i][1].start()
+            for j in range(group):
+                @pl.when(slot == j)
+                def _():
+                    for q in range(CHUNKS):
                         run(row_copies(step, j, q), "start")
-
-        for q in range(CHUNKS):
-            relay_col(step, q)
-            if q + 1 < CHUNKS:
-                relay_row(step, q)
+                    twin_copy(step, j).start()
+
+        relay_col(step)
+        for q in range(CHUNKS - 1):
+            relay_row(step, q)
+        settle_col(step)
+
+        @pl.when((step > 0) & jnp.logical_not(on_diag))
+        def _():
+            receive_rows(step - 1)
 
         for j in range(group):
             rows = pl.ds(j * width, width)
@@ -193,6 +238,10 @@
 
             run(g_copies(step, j), "start")
         relay_row(step, CHUNKS - 1)
+        for j in range(group):
+            @pl.when(jnp.logical_not(on_lane(j)))
+            def _():
+                twin_copy(step, j).wait_recv()
 
         for j in [0, group - 1] + list(range(1, group - 1)):
             rows = pl.ds(j * width, width)
@@ -237,28 +286,28 @@
             elif j == group - 1:
                 run(h_copies(step)[:1], "start")
 
-        copies = h_copies(step)
-
-        @pl.when(row < row_count - 1)
-        def _():
-            copies[1][1].wait_recv()
-            o_ref[pl.ds((2 * group - 1) * half, half), :] = hin[step, 1].astype(jnp.float32)
-
-        @pl.when(row > 0)
-        def _():
-            copies[0][1].wait_recv()
-            o_ref[pl.ds(0, half), :] = hin[step, 0].astype(jnp.float32)
-
-        for q in range(CHUNKS):
+        @pl.when((step < STEPS - 1) & on_diag)
+        def _():
+            receive_rows(step)
+            solve(step + 1)
+
+        return carry
+
+    lax.fori_loop(0, STEPS, one_step, 0)
+    receive_rows(STEPS - 1)
+
+    def drain(step, carry):
+        for q in range(parts):
             run(col_copies(step, q), "wait_send")
-            for j in range(group):
+        for j in range(group):
+            for q in range(CHUNKS):
                 run(row_copies(step, j, q), "wait_send")
-        for j in range(group):
+            act(on_lane(j), twin_copy(step, j), "wait_send")
             run(g_copies(step, j), "wait_send")
-        run(copies, "wait_send")
+        run(h_copies(step), "wait_send")
         return carry
 
-    lax.fori_loop(0, STEPS, one_step, 0)
+    lax.fori_loop(0, STEPS, drain, 0)
 
 
 def shards(factor):
@@ -269,6 +318,7 @@
     pair_count = lax.axis_size("col")
     bits = row_count.bit_length() - 1
     low = jnp.bfloat16
+    parts = PARTS * (1 << (bits - 1).bit_length())
     dma = pltpu.SemaphoreType.DMA
     return pl.pallas_call(
         functools.partial(kernel, row_count, pair_count),
@@ -283,10 +333,12 @@
             pltpu.VMEM((STEPS, 2, half, width), low),
             pltpu.VMEM((STEPS, 2, half, width), low),
             dma,
-            dma((STEPS, CHUNKS, bits)),
-            dma((STEPS, CHUNKS)),
-            dma((STEPS, group, CHUNKS, 3)),
+            dma((STEPS, parts, bits)),
+            dma((STEPS, parts)),
+            dma((STEPS, group, CHUNKS, 2)),
             dma((STEPS, group, CHUNKS)),
+            dma((STEPS, group)),
+            dma((STEPS, group)),
             dma((STEPS, group, 2)),
             dma((STEPS, group, 2)),
             dma((STEPS, 2)),

time: 98.5 us -> 83 us (0.84)
  the two profiles are of different devices: /device:TPU:6 before, /device:TPU:5 now
where the time goes in v1:
time: 83 us; the launch traced here: 82.8 us
  Pallas kernels  79.7 us (96%)
  local copies, waits for them, and re-layouts  3.08 us (4%)
    pallas_call x1, Pallas kernels, shards(): pl.pallas_call(functools.partial(kernel, row_count, pair_count), out_shap...  79.7 us
    unnamed x1, local copies, waits for them, and re-layouts  3.08 us

profile of v1, /device:TPU:5, one launch (start us, length us, event | category | flops | bytes accessed | tf_op | source)
XLA Modules:
  0.0 82.8 jit_solution(6528025275999201496)
XLA Ops:
  0.0 79.7 %shard_map.17 = f32[1024,512]{1,0:T(8,128)} custom-call(f32[1024,512]{1,0:T(8,128)} %x_ref.1), custom_call_target="tpu_custom_call" | custom-call | tf_op jit(solution)/shard_map/pallas_call | solution.py:323
  79.7 3.1 %copy.3 = f32[1024,512]{1,0:T(8,128)} copy(f32[1024,512]{1,0:T(8,128)} %shard_map.17) | data formatting | bytes 4194304

commit v2 on v1

--- a/solution.py
+++ b/solution.py
@@ -10,7 +10,7 @@
 
 SWEEPS = 2
 STEPS = 2
-CHUNKS = 4
+CHUNKS = 8
 PARTS = 1
 MESH = pl.DeviceIdType.MESH
 
@@ -128,14 +128,14 @@
                     grecv.at[step, j, 1], {"col": col - 1})),
         ]
 
-    def h_copies(step):
+    def h_copies(step, side):
         return [
             (row + 1 < row_count,
-             remote(hout.at[step, 0], hin.at[step, 0], hsend.at[step, 0], hrecv.at[step, 0],
-                    {"row": row + 1})),
+             remote(hout.at[step, 0, side], hin.at[step, 0, side], hsend.at[step, 0, side],
+                    hrecv.at[step, 0, side], {"row": row + 1})),
             (row > 0,
-             remote(hout.at[step, 1], hin.at[step, 1], hsend.at[step, 1], hrecv.at[step, 1],
-                    {"row": row - 1})),
+             remote(hout.at[step, 1, side], hin.at[step, 1, side], hsend.at[step, 1, side],
+                    hrecv.at[step, 1, side], {"row": row - 1})),
         ]
 
     def run(copies, what):
@@ -168,17 +168,19 @@
                     twin_copy(step, j).start()
 
     def receive_rows(step):
-        copies = h_copies(step)
-
-        @pl.when(row < row_count - 1)
-        def _():
-            copies[1][1].wait_recv()
-            o_ref[pl.ds((2 * group - 1) * half, half), :] = hin[step, 1].astype(jnp.float32)
-
-        @pl.when(row > 0)
-        def _():
-            copies[0][1].wait_recv()
-            o_ref[pl.ds(0, half), :] = hin[step, 0].astype(jnp.float32)
+        for side in range(2):
+            copies = h_copies(step, side)
+            cols = pl.ds(side * half, half)
+
+            @pl.when(row < row_count - 1)
+            def _():
+                copies[1][1].wait_recv()
+                o_ref[pl.ds((2 * group - 1) * half, half), cols] = hin[step, 1, side].astype(jnp.float32)
+
+            @pl.when(row > 0)
+            def _():
+                copies[0][1].wait_recv()
+                o_ref[pl.ds(0, half), cols] = hin[step, 0, side].astype(jnp.float32)
 
     def solve(step):
         rotation = inner_solve(o_ref[pl.ds(pl.multiple_of(slot * width, width), width), :])
@@ -268,7 +270,7 @@
                     @pl.when(row > 0)
                     def _():
                         put(2, upper)
-                        hout[step, 1, :, cols] = lower.astype(jnp.bfloat16)
+                        hout[step, 1, side] = lower.astype(jnp.bfloat16)
                 else:
                     put(2 * j - 1, lower)
                     if j < group - 1:
@@ -280,11 +282,11 @@
 
                         @pl.when(row < row_count - 1)
                         def _():
-                            hout[step, 0, :, cols] = upper.astype(jnp.bfloat16)
-            if j == 0:
-                run(h_copies(step)[1:], "start")
-            elif j == group - 1:
-                run(h_copies(step)[:1], "start")
+                            hout[step, 0, side] = upper.astype(jnp.bfloat16)
+                if j == 0:
+                    run(h_copies(step, side)[1:], "start")
+                elif j == group - 1:
+                    run(h_copies(step, side)[:1], "start")
 
         @pl.when((step < STEPS - 1) & on_diag)
         def _():
@@ -304,7 +306,8 @@
                 run(row_copies(step, j, q), "wait_send")
             act(on_lane(j), twin_copy(step, j), "wait_send")
             run(g_copies(step, j), "wait_send")
-        run(h_copies(step), "wait_send")
+        for side in range(2):
+            run(h_copies(step, side), "wait_send")
         return carry
 
     lax.fori_loop(0, STEPS, drain, 0)
@@ -330,8 +333,8 @@
             pltpu.VMEM((STEPS, group, width, width), low),
             pltpu.VMEM((STEPS, 2, rows, half), low),
             pltpu.VMEM((STEPS, 2, rows, half), low),
-            pltpu.VMEM((STEPS, 2, half, width), low),
-            pltpu.VMEM((STEPS, 2, half, width), low),
+            pltpu.VMEM((STEPS, 2, 2, half, half), low),
+            pltpu.VMEM((STEPS, 2, 2, half, half), low),
             dma,
             dma((STEPS, parts, bits)),
             dma((STEPS, parts)),
@@ -341,11 +344,11 @@
             dma((STEPS, group)),
             dma((STEPS, group, 2)),
             dma((STEPS, group, 2)),
-            dma((STEPS, 2)),
-            dma((STEPS, 2)),
+            dma((STEPS, 2, 2)),
+            dma((STEPS, 2, 2)),
         ],
         compiler_params=pltpu.CompilerParams(
-            collective_id=0, has_side_effects=True, vmem_limit_bytes=56 * 1024 * 1024
+            collective_id=0, has_side_effects=True, vmem_limit_bytes=24 * 1024 * 1024
         ),
     )(factor)
 

time: 83 us -> 77.6 us (0.935)
  Pallas kernels: 79.7 us -> 74.5 us
    pallas_call x1, Pallas kernels: 79.7 us -> 74.5 us  [shards(): pl.pallas_call(functools.partial(kernel, row_count, pair_count), out_shap...]
    unnamed x1 -> x3, local copies, waits for them, and re-layouts: 3.08 us -> 2.91 us
where the time goes in v2:
time: 77.6 us; the launch traced here: 77.4 us
  Pallas kernels  74.5 us (96%)
  local copies, waits for them, and re-layouts  2.91 us (4%)
    pallas_call x1, Pallas kernels, shards(): pl.pallas_call(functools.partial(kernel, row_count, pair_count), out_shap...  74.5 us
    unnamed x3, local copies, waits for them, and re-layouts  2.91 us

profile of v2, /device:TPU:5, one launch (start us, length us, event | category | flops | bytes accessed | tf_op | source)
XLA Modules:
  0.0 77.4 jit_solution(7700825530510999599)
XLA Ops:
  0.0 0.0 copy-start
  0.0 1.6 %copy-done = f32[1024,512]{1,0:T(8,128)S(1)} copy-done((f32[1024,512]{1,0:T(8,128)S(1)}, f32[1024,512]{1,0:T(8,128)}, u32[]{:S(2)}) %copy-start) | copy-done | bytes 2097176
  1.6 74.5 %shard_map.17 = f32[1024,512]{1,0:T(8,128)S(1)} custom-call(f32[1024,512]{1,0:T(8,128)S(1)} %copy-done), custom_call_target="tpu_custom_call" | custom-call | tf_op jit(solution)/shard_map/pallas_call | solution.py:326
  76.1 1.3 %copy.3 = f32[1024,512]{1,0:T(8,128)} copy(f32[1024,512]{1,0:T(8,128)S(1)} %shard_map.17) | data formatting | bytes 4194304
Async XLA Ops:
  0.0 1.6 %copy-start = (f32[1024,512]{1,0:T(8,128)S(1)}, f32[1024,512]{1,0:T(8,128)}, u32[]{:S(2)}) copy-start(f32[1024,512]{1,0:T(8,128)} %x_ref.1) | copy-start | bytes 6291460
